TPU v7x, 768 devices: a whole 4x8x12 slice. The times are simulated.
768 devices in a mesh: dp: 96 (over x, z, y_lo), tensor: 8 (over y_hi, core).
Axes of the slice: x: 4, y: 8 (y_hi: 4, y_lo: 2; y = y_hi * 2 + y_lo), z: 12, core: 2. Of those that a mesh axis runs over, the one named last changes fastest.
Arguments:
- x_saved: bfloat16 [24576, 2688], P(('dp', 'tensor')), may hold values from -24 to 24
- block_scales: float32 [24576, 21], P(('dp', 'tensor')), may hold values from 0.25 to 4
- gate_grad: bfloat16 [24576, 12800], P('dp', 'tensor'), may hold values from -6 to 6
- gate_weight: bfloat16 [2688, 12800], P(None, 'tensor'), may hold values from -0.125 to 0.125
Outputs:
- input_grad: bfloat16 [24576, 2688], P(('dp', 'tensor'))
- weight_grad: float32 [2688, 12800], P('dp', 'tensor')
All inputs are finite; a program needn't handle non-finite values.
Results may differ from a plain program's by a relative error of at most 0.0029.
Values may be sent and summed in bfloat16 or wider, within the bound.
A program may use at most 128 MiB of HBM per device.

v0:
```python
import math

import jax
import jax.numpy as jnp
from jax import lax
from jax.sharding import PartitionSpec as P


def scaled_inputs(x_saved, block_scales):
    local_rows, model_width = x_saved.shape
    block_count = block_scales.shape[1]
    scaled = (
        x_saved.astype(jnp.float32).reshape(local_rows, block_count, model_width // block_count)
        * block_scales[:, :, None]
    )
    return scaled.reshape(local_rows, model_width).astype(jnp.bfloat16)


def shards(x_saved, block_scales, gate_grad, gate_weight):
    group_rows, hidden_units = gate_grad.shape
    total_tokens = group_rows * lax.axis_size("dp")
    inputs = scaled_inputs(x_saved, block_scales)
    group_inputs = lax.all_gather(inputs, "tensor", axis=0, tiled=True)
    contract_tokens = (((0,), (0,)), ((), ()))
    contract_hidden = (((1,), (1,)), ((), ()))
    summed = lax.psum_scatter(
        lax.dot_general(
            group_inputs, gate_grad, contract_tokens, preferred_element_type=jnp.float32
        ),
        "dp",
        scatter_dimension=0,
        tiled=True,
    )
    weight_grad = summed / math.sqrt(total_tokens)
    input_sum = lax.psum_scatter(
        lax.dot_general(
            gate_grad, gate_weight, contract_hidden, preferred_element_type=jnp.float32
        ),
        "tensor",
        scatter_dimension=0,
        tiled=True,
    )
    return (input_sum.astype(jnp.bfloat16), weight_grad)


def solution(mesh):
    return jax.shard_map(
        shards,
        mesh=mesh,
        in_specs=(
            P(("dp", "tensor"), None),
            P(("dp", "tensor"), None),
            P("dp", "tensor"),
            P(None, "tensor"),
        ),
        out_specs=(P(("dp", "tensor"), None), P("dp", "tensor")),
        check_vma=False,
    )
```

profile of v0, /device:TPU:12, one launch (start us, length us, event | category | flops | bytes accessed | tf_op | source)
XLA Modules:
  0.0 739.3 jit_solution(1237692151448283366)
XLA Ops:
  7.2 0.8 copy.8
  8.1 0.2 mul.11
  8.2 1.7 fusion.1
  9.9 0.0 reduce-scatter.4.cloned.1.call-start
  10.0 7.7 %fusion.2 = f32[256,2688]{1,0:T(8,128)} fusion(bf16[256,1600]{0,1:T(8,128)(2,1)S(1)} %copy-done, bf16[2688,1600]{0,1:T(8,128)(2,1)} %param.7), kind=kOutput, calls=%fused_computation.3 | convolution fusion | flops 2202009600 | bytes 12173312 | tf_op jit(solution)/shard_map/dot_general | solution.py:36
  17.7 36.8 %all-gather.2.cloned.1.call-done = bf16[256,2688]{1,0:T(8,128)(2,1)} async-done(((bf16[32,2688]{1,0:T(8,128)(2,1)}), bf16[256,2688]{1,0:T(8,128)(2,1)}) %all-gather.2.cloned.1.call-update) | async-done | bytes 1376272 | tf_op jit(solution)/shard_map/all_gather | solution.py:23
  54.5 10.2 %fusion.3 = f32[2688,1600]{1,0:T(8,128)} fusion(bf16[256,2688]{1,0:T(8,128)(2,1)} %all-gather.2.cloned.1.call-done, bf16[256,1600]{0,1:T(8,128)(2,1)S(1)} %copy-done), kind=kOutput, calls=%fused_computation.4 | convolution fusion | flops 2202009600 | bytes 19398656 | tf_op jit(solution)/shard_map/dot_general | solution.py:27
  64.7 467.8 %fusion = f32[32,1600]{1,0:T(8,128)S(1)} fusion(f32[2688,1600]{1,0:T(8,128)} %fusion.3), kind=kCustom, calls=%all-reduce-scatter | all-reduce-scatter fusion | flops 4915201 | bytes 17412096
  532.5 4.5 collective-permute-start
  537.1 10.2 %collective-permute-start.11 = (f32[28,1600]{1,0:T(8,128)S(1)}, f32[28,1600]{1,0:T(8,128)S(1)}, u32[]{:S(2)}, u32[]{:S(2)}) collective-permute-start(f32[28,1600]{1,0:T(8,128)S(1)} %slice), channel_id=1, source_target_pairs={{0,96},{8,104},{16,112},{24,120},{32,128},{40,136},{48,144},{56,15... | collective-permute-start | bytes 537608
  547.3 1.9 collective-permute-start.1
  549.3 5.5 collective-permute-start.10
  554.8 2.9 collective-permute-start.2
  557.7 6.1 collective-permute-done.11
  563.8 1.9 collective-permute-start.3
  565.7 4.8 collective-permute-start.4
  570.6 20.5 %collective-permute-done.1 = f32[32,1600]{1,0:T(8,128)S(1)} collective-permute-done((f32[32,1600]{1,0:T(8,128)S(1)}, f32[32,1600]{1,0:T(8,128)S(1)}, u32[]{:S(2)}, u32[]{:S(2)}) %collective-permute-start.1) | collective-permute-done | bytes 204832
  591.1 1.9 collective-permute-start.5
  593.0 1.9 collective-permute-start.6
  594.9 7.3 collective-permute-done.2
  602.3 1.9 collective-permute-start.7
  604.2 8.7 %collective-permute-start.8 = (f32[32,1600]{1,0:T(8,128)S(1)}, f32[32,1600]{1,0:T(8,128)S(1)}, u32[]{:S(2)}, u32[]{:S(2)}) collective-permute-start(f32[32,1600]{1,0:T(8,128)S(1)} %fusion), channel_id=1, source_target_pairs={{0,72},{8,80},{16,88},{24,96},{32,104},{40,112},{48,120},{56,128},... | collective-permute-start | bytes 614408
  612.9 1.9 collective-permute-done.4
  614.8 2.9 collective-permute-start.9
  617.6 1.3 dynamic-slice.4
  619.6 15.0 %collective-permute-done.5 = f32[32,1600]{1,0:T(8,128)S(1)} collective-permute-done((f32[32,1600]{1,0:T(8,128)S(1)}, f32[32,1600]{1,0:T(8,128)S(1)}, u32[]{:S(2)}, u32[]{:S(2)}) %collective-permute-start.5) | collective-permute-done | bytes 204832
  634.6 10.0 %collective-permute-done.6 = f32[32,1600]{1,0:T(8,128)S(1)} collective-permute-done((f32[32,1600]{1,0:T(8,128)S(1)}, f32[32,1600]{1,0:T(8,128)S(1)}, u32[]{:S(2)}, u32[]{:S(2)}) %collective-permute-start.6) | collective-permute-done | bytes 204832
  644.6 40.7 %collective-permute-done.8 = f32[32,1600]{1,0:T(8,128)S(1)} collective-permute-done((f32[32,1600]{1,0:T(8,128)S(1)}, f32[32,1600]{1,0:T(8,128)S(1)}, u32[]{:S(2)}, u32[]{:S(2)}) %collective-permute-start.8) | collective-permute-done | bytes 204832
  685.3 24.0 %collective-permute-done.9 = f32[32,1600]{1,0:T(8,128)} collective-permute-done((f32[32,1600]{1,0:T(8,128)S(1)}, f32[32,1600]{1,0:T(8,128)}, u32[]{:S(2)}, u32[]{:S(2)}) %collective-permute-start.9) | collective-permute-done | bytes 204832
  709.3 19.8 %concatenate = f32[412,1600]{1,0:T(8,128)} concatenate(f32[28,1600]{1,0:T(8,128)S(1)} %collective-permute-done.11, f32[32,1600]{1,0:T(8,128)S(1)} %collective-permute-done.10, f32[32,1600]{1,0:T(8,128)} %collective-permute-done.9, f32[32,1600]{1,0:T(8,128)S(1)} %collective-permute-done.8, f32[32,1600]{1,0:T(8,128)S(1)} %collective-permute-done.7, ...), dimensions={0} | concatenate | bytes 5273600
  729.1 1.7 dynamic-slice_multiply_fusion
  730.8 1.7 convert_element_type.9
  (11 shorter events, 0.1 us)
Async XLA Ops:
  7.2 2.8 copy-start
  7.2 47.4 %all-gather.2.cloned.1.call-start = ((), (), s32[]{:S(2)}) async-start(), calls=%async_computation.2 | async-start | bytes 1548288 | tf_op jit(solution)/shard_map/all_gather | solution.py:23
  9.9 720.9 %reduce-scatter.4.cloned.1.call-start = ((), (), s32[]{:S(2)}) async-start(), calls=%async_computation.1 | async-start | bytes 3096576 | tf_op jit(solution)/shard_map/reduce_scatter | solution.py:35
  532.5 33.2 %collective-permute-start = (f32[32,1600]{1,0:T(8,128)S(1)}, f32[32,1600]{1,0:T(8,128)S(1)}, u32[]{:S(2)}, u32[]{:S(2)}) collective-permute-start(f32[32,1600]{1,0:T(8,128)S(1)} %fusion), channel_id=1, source_target_pairs={{0,8},{8,16},{16,24},{24,32},{32,40},{40,48},{48,56},{56,64},{64,7... | collective-permute-start | bytes 614408
  537.1 26.7 %collective-permute-start.11 = (f32[28,1600]{1,0:T(8,128)S(1)}, f32[28,1600]{1,0:T(8,128)S(1)}, u32[]{:S(2)}, u32[]{:S(2)}) collective-permute-start(f32[28,1600]{1,0:T(8,128)S(1)} %slice), channel_id=1, source_target_pairs={{0,96},{8,104},{16,112},{24,120},{32,128},{40,136},{48,144},{56,15... | collective-permute-start | bytes 537608
  547.3 43.8 %collective-permute-start.1 = (f32[32,1600]{1,0:T(8,128)S(1)}, f32[32,1600]{1,0:T(8,128)S(1)}, u32[]{:S(2)}, u32[]{:S(2)}) collective-permute-start(f32[32,1600]{1,0:T(8,128)S(1)} %fusion), channel_id=1, source_target_pairs={{0,16},{8,24},{16,32},{24,40},{32,48},{40,56},{48,64},{56,72},{64,... | collective-permute-start | bytes 614408
  549.3 43.8 %collective-permute-start.10 = (f32[32,1600]{1,0:T(8,128)S(1)}, f32[32,1600]{1,0:T(8,128)S(1)}, u32[]{:S(2)}, u32[]{:S(2)}) collective-permute-start(f32[32,1600]{1,0:T(8,128)S(1)} %fusion), channel_id=1, source_target_pairs={{0,88},{8,96},{16,104},{24,112},{32,120},{40,128},{48,136},{56,144... | collective-permute-start | bytes 614408
  554.8 47.5 %collective-permute-start.2 = (f32[32,1600]{1,0:T(8,128)S(1)}, f32[32,1600]{1,0:T(8,128)S(1)}, u32[]{:S(2)}, u32[]{:S(2)}) collective-permute-start(f32[32,1600]{1,0:T(8,128)S(1)} %fusion), channel_id=1, source_target_pairs={{0,24},{8,32},{16,40},{24,48},{32,56},{40,64},{48,72},{56,80},{64,... | collective-permute-start | bytes 614408
  563.8 40.4 %collective-permute-start.3 = (f32[32,1600]{1,0:T(8,128)S(1)}, f32[32,1600]{1,0:T(8,128)S(1)}, u32[]{:S(2)}, u32[]{:S(2)}) collective-permute-start(f32[32,1600]{1,0:T(8,128)S(1)} %fusion), channel_id=1, source_target_pairs={{0,32},{8,40},{16,48},{24,56},{32,64},{40,72},{48,80},{56,88},{64,... | collective-permute-start | bytes 614408
  565.7 49.0 %collective-permute-start.4 = (f32[32,1600]{1,0:T(8,128)S(1)}, f32[32,1600]{1,0:T(8,128)S(1)}, u32[]{:S(2)}, u32[]{:S(2)}) collective-permute-start(f32[32,1600]{1,0:T(8,128)S(1)} %fusion), channel_id=1, source_target_pairs={{0,40},{8,48},{16,56},{24,64},{32,72},{40,80},{48,88},{56,96},{64,... | collective-permute-start | bytes 614408
  591.1 43.5 %collective-permute-start.5 = (f32[32,1600]{1,0:T(8,128)S(1)}, f32[32,1600]{1,0:T(8,128)S(1)}, u32[]{:S(2)}, u32[]{:S(2)}) collective-permute-start(f32[32,1600]{1,0:T(8,128)S(1)} %fusion), channel_id=1, source_target_pairs={{0,48},{8,56},{16,64},{24,72},{32,80},{40,88},{48,96},{56,104},{64... | collective-permute-start | bytes 614408
  593.0 51.6 %collective-permute-start.6 = (f32[32,1600]{1,0:T(8,128)S(1)}, f32[32,1600]{1,0:T(8,128)S(1)}, u32[]{:S(2)}, u32[]{:S(2)}) collective-permute-start(f32[32,1600]{1,0:T(8,128)S(1)} %fusion), channel_id=1, source_target_pairs={{0,56},{8,64},{16,72},{24,80},{32,88},{40,96},{48,104},{56,112},{6... | collective-permute-start | bytes 614408
  602.3 42.3 %collective-permute-start.7 = (f32[32,1600]{1,0:T(8,128)S(1)}, f32[32,1600]{1,0:T(8,128)S(1)}, u32[]{:S(2)}, u32[]{:S(2)}) collective-permute-start(f32[32,1600]{1,0:T(8,128)S(1)} %fusion), channel_id=1, source_target_pairs={{0,64},{8,72},{16,80},{24,88},{32,96},{40,104},{48,112},{56,120},{... | collective-permute-start | bytes 614408
  604.2 81.1 %collective-permute-start.8 = (f32[32,1600]{1,0:T(8,128)S(1)}, f32[32,1600]{1,0:T(8,128)S(1)}, u32[]{:S(2)}, u32[]{:S(2)}) collective-permute-start(f32[32,1600]{1,0:T(8,128)S(1)} %fusion), channel_id=1, source_target_pairs={{0,72},{8,80},{16,88},{24,96},{32,104},{40,112},{48,120},{56,128},... | collective-permute-start | bytes 614408
  614.8 94.5 %collective-permute-start.9 = (f32[32,1600]{1,0:T(8,128)S(1)}, f32[32,1600]{1,0:T(8,128)}, u32[]{:S(2)}, u32[]{:S(2)}) collective-permute-start(f32[32,1600]{1,0:T(8,128)S(1)} %fusion), channel_id=1, source_target_pairs={{0,80},{8,88},{16,96},{24,104},{32,112},{40,120},{48,128},{56,136}... | collective-permute-start | bytes 614408
Sparse Core Ops, SparseCore 0:
  11.0 43.4 all-gather.1
  57.7 93.9 reduce-scatter.3
where the time goes:
time: 741 us; the launch traced here: 739 us
  blocking collectives  468 us (63%)
  waiting for transfers between devices  162 us (22%)
  starting transfers between devices  49.2 us (7%)
  local copies, waits for them, and re-layouts  22.1 us (3%)
  matrix products  17.9 us (2%)
  between operations  14.9 us (2%)
    unnamed x1, blocking collectives  468 us
    unnamed x14, waiting for transfers between devices  126 us
    unnamed x12, starting transfers between devices  49.2 us
    all_gather x1, waiting for transfers between devices, shards(): group_inputs = lax.all_gather(inputs, 'tensor', axis=0, tiled=True)  36.8 us
    unnamed x6, local copies, waits for them, and re-layouts  22 us
  transfers between devices with their start and end apart: 14, of which 9 were waited for; matrix products, arithmetic and copies ran while one was open for 69% of the time, Pallas kernels for 0%

commit v1 on v0

v1 whole, which is shorter than its diff:
```python
import functools
import math

import jax
import jax.numpy as jnp
from jax import lax
from jax.experimental import pallas as pl
from jax.experimental.pallas import tpu as pltpu
from jax.sharding import PartitionSpec as P

MESH = pl.DeviceIdType.MESH
F32, BF16 = jnp.float32, jnp.bfloat16

NX, NZ, NL, NY, NC = 4, 12, 2, 4, 2
D, FF = 2688, 1600
ROWS = 32
GROUP = 256
DX = D // NX
DZ = DX // NZ
BLOCK = 128
PIECES = ((0, 512), (512, 512), (1024, 256), (1280, 320))
FWD, BWD = 6, 5
WCHUNK = 384


def kernel(x_ref, scale_ref, grad_ref, weight_ref, ig_ref, wg_ref, *scratch):
    (pack, a_buf, a_t, g_buf, w_buf, part, ig_part, ig_core, ig_send, ig_recv) = scratch[:10]
    n = len(PIECES)
    zf0, zb0 = scratch[10:10 + n], scratch[10 + n:10 + 2 * n]
    zf, zb = scratch[10 + 2 * n:10 + 3 * n], scratch[10 + 3 * n:10 + 4 * n]
    zl, lsend, lrecv = (scratch[10 + k * n:10 + (k + 1) * n] for k in (4, 5, 6))
    (load_sem, a2a_s, a2a_r, ya_s, ya_r, ca_s, ca_r, g_s, g_r, ic_s, ic_r, iy_s, iy_r,
     zf_s, zf_r, zb_s, zb_r, l_s, l_r) = scratch[10 + 7 * n:]

    dp, tensor = lax.axis_index("dp"), lax.axis_index("tensor")
    x, z, yl = dp // (NZ * NL), (dp // NL) % NZ, dp % NL
    yh, c = tensor // NC, tensor % NC
    s = 1 - 2 * c

    def at(x=x, z=z, yl=yl, yh=yh, c=c):
        return ((x * NZ + z) * NL + yl, yh * NC + c)

    x_to, x_from, x_opp = (x + s + NX) % NX, (x - s + NX) % NX, (x + 2) % NX
    y_to, y_from, y_opp = (yh + s + NY) % NY, (yh - s + NY) % NY, (yh + 2) % NY
    z_to, z_from = (z + s + NZ) % NZ, (z - s + NZ) % NZ
    mate = at(c=1 - c)

    pending = []

    def send(src, dst, send_sem, recv_sem, device):
        copy = pltpu.make_async_remote_copy(
            src_ref=src, dst_ref=dst, send_sem=send_sem, recv_sem=recv_sem,
            device_id=device, device_id_type=MESH,
        )
        copy.start()
        pending.append(copy)

    def arrived(dst, sem):
        pltpu.make_async_copy(dst, dst, sem).wait()

    own_grad = pltpu.make_async_copy(grad_ref, g_buf.at[x], load_sem.at[0])
    own_grad.start()
    weights = []
    for k in range(D // WCHUNK):
        rows = pl.ds(k * WCHUNK, WCHUNK)
        load = pltpu.make_async_copy(weight_ref.at[rows], w_buf.at[rows], load_sem.at[1 + k])
        load.start()
        weights.append(load)

    barrier = pltpu.get_barrier_semaphore()
    partners = [at(x=x_to), at(x=x_from), at(x=x_opp), at(yh=y_to), at(yh=y_from), at(yh=y_opp),
                at(z=z_to), at(z=z_from), at(yl=1 - yl), mate]
    for partner in partners:
        pl.semaphore_signal(barrier, inc=1, device_id=partner, device_id_type=MESH)

    scaled = jnp.concatenate(
        [x_ref[:, b * BLOCK:(b + 1) * BLOCK].astype(F32) * scale_ref[:, b:b + 1] for b in range(D // BLOCK)],
        axis=1,
    ).astype(BF16).astype(F32)
    for k in range(NX):
        pack[k] = scaled[:, k * DX:(k + 1) * DX].astype(BF16)
    pl.semaphore_wait(barrier, len(partners))

    def token_rows(yh, c):
        return pl.ds(pl.multiple_of((yh * NC + c) * ROWS, ROWS), ROWS)

    mine = token_rows(yh, c)
    for k, target in enumerate((x_to, x_from, x_opp)):
        send(pack.at[target], a_buf.at[x, mine], a2a_s.at[k], a2a_r.at[k], at(x=target))
    a_buf[x, mine] = pack[x]

    def grad_own(i):
        cols = pl.ds(*PIECES[i])
        for k, target in enumerate((x_to, x_from)):
            send(grad_ref.at[:, cols], g_buf.at[x, :, cols], g_s.at[3 * i + k], g_r.at[3 * i + k], at(x=target))

    def grad_forward(i):
        cols = pl.ds(*PIECES[i])
        block = g_buf.at[x_from, :, cols]
        arrived(block, g_r.at[3 * i])
        send(block, block, g_s.at[3 * i + 2], g_r.at[3 * i + 2], at(x=x_to))

    def grad_rest(i):
        cols = pl.ds(*PIECES[i])
        arrived(g_buf.at[x_to, :, cols], g_r.at[3 * i + 1])
        arrived(g_buf.at[x_opp, :, cols], g_r.at[3 * i + 2])

    grad_own(0)
    grad_own(1)

    for k, source in enumerate((x_from, x_to, x_opp)):
        arrived(a_buf.at[source, mine], a2a_r.at[k])
    for k, target in enumerate((y_to, y_from)):
        block = a_buf.at[:, mine]
        send(block, block, ya_s.at[k], ya_r.at[k], at(yh=target))
    send(a_buf.at[:, mine], a_buf.at[:, mine], ca_s.at[0], ca_r.at[0], mate)

    own_grad.wait()

    def ig_chunk(k):
        weights[k].wait()
        rows = pl.ds(k * WCHUNK, WCHUNK)
        prod = lax.dot_general(
            g_buf[x], w_buf[rows, :], (((1,), (1,)), ((), ())), preferred_element_type=F32
        )
        ig_part[:, :, rows] = prod.reshape(NY * NC, ROWS, WCHUNK)

    for k in range(4):
        ig_chunk(k)

    def from_y(k, source):
        block = a_buf.at[:, token_rows(source, c)]
        arrived(block, ya_r.at[k])
        send(block, block, ca_s.at[1 + k], ca_r.at[1 + k], mate)
        return block

    block = from_y(0, y_from)
    send(block, block, ya_s.at[2], ya_r.at[2], at(yh=y_to))
    grad_forward(0)
    grad_own(2)
    for k in range(4, D // WCHUNK):
        ig_chunk(k)
    for k in range(NY):
        other = (yh + k) % NY
        send(ig_part.at[other * NC + 1 - c], ig_core.at[other], ic_s.at[k], ic_r.at[k], mate)
    from_y(1, y_to)
    for k in range(NY):
        arrived(ig_core.at[(yh + k) % NY], ic_r.at[k])
    for k in range(1, NY):
        other = (yh + k) % NY
        ig_send[k - 1] = (ig_part[other * NC + c] + ig_core[other]).astype(BF16)
        send(ig_send.at[k - 1], ig_recv.at[k - 1], iy_s.at[k - 1], iy_r.at[k - 1], at(yh=other))

    grad_forward(1)
    grad_own(3)
    from_y(2, y_opp)
    for k, source in enumerate((yh, y_to, y_from, y_opp)):
        arrived(a_buf.at[:, token_rows(source, 1 - c)], ca_r.at[k])
    for k in range(NX):
        a_t[:, k * GROUP:(k + 1) * GROUP] = a_buf[k].astype(F32).T.astype(BF16)

    def multiply(i):
        start, width = PIECES[i]
        grad_rest(i)
        for first in range(0, width, 256):
            cols = pl.ds(start + first, min(256, width - first))
            rhs = jnp.concatenate([g_buf[k, :, cols] for k in range(NX)], axis=0)
            part[:, cols] = jnp.dot(a_t[...], rhs, preferred_element_type=F32)

    def own_part(i, owner):
        return part[pl.ds(pl.multiple_of(owner * DZ, 8), DZ), pl.ds(*PIECES[i])]

    def step(i, j):
        chains = (
            (FWD, z_to, (z + s * (FWD - j) + NZ) % NZ, zf0[i], zf[i], zl[i].at[0], zl[i].at[2], zf_s, zf_r),
            (BWD, z_from, (z - s * (BWD - j) + NZ) % NZ, zb0[i], zb[i], zl[i].at[1], zl[i].at[3], zb_s, zb_r),
        )
        for hops, target, owner, first, slots, last_out, last_in, ss, rs in chains:
            if j >= hops:
                continue
            value = own_part(i, owner)
            if j > 0:
                arrived(slots.at[j - 1], rs.at[i * hops + j - 1])
                value = value + slots[j - 1].astype(F32)
            if j == hops - 1:
                last_out[...] = value
                src, dst = last_out, last_in
            elif j == 0:
                first[...] = value.astype(BF16)
                src, dst = first, slots.at[0]
            else:
                slots[j - 1] = value.astype(BF16)
                src, dst = slots.at[j - 1], slots.at[j]
            send(src, dst, ss.at[i * hops + j], rs.at[i * hops + j], at(z=target))

    def close(i):
        arrived(zl[i].at[2], zf_r.at[i * FWD + FWD - 1])
        arrived(zl[i].at[3], zb_r.at[i * BWD + BWD - 1])
        lsend[i][...] = own_part(i, z) + zl[i][2] + zl[i][3]
        rows = pl.ds(pl.multiple_of((1 - yl) * 24, 8), 32)
        send(lsend[i].at[rows], lrecv[i], l_s.at[i], l_r.at[i], at(yl=1 - yl))

    def finish(i):
        arrived(lrecv[i], l_r.at[i])
        rows = pl.ds(pl.multiple_of(yl * 24, 8), 32)
        total = (lsend[i][rows, :] + lrecv[i][...]) * (1.0 / math.sqrt(GROUP * NX * NZ * NL))
        wg_ref[:, pl.ds(*PIECES[i])] = jnp.where(yl == 0, total[:28], total[4:])

    def work(i, j):
        if j < 0:
            return
        if j == 0:
            multiply(i)
        if j < FWD:
            step(i, j)
        if j == FWD:
            close(i)
        if j == FWD + 1:
            finish(i)

    def input_grad():
        total = ig_part[yh * NC + c] + ig_core[yh]
        for k in range(1, NY):
            arrived(ig_recv.at[k - 1], iy_r.at[k - 1])
            total = total + ig_recv[k - 1].astype(F32)
        ig_ref[...] = total.astype(BF16)

    offsets = (0, 1, 2, 3)
    for tick in range(FWD + 2 + offsets[-1]):
        if tick == 2:
            grad_forward(2)
        if tick == 3:
            grad_forward(3)
        if tick == 6:
            input_grad()
        for i in range(len(PIECES)):
            if tick - offsets[i] < FWD + 2:
                work(i, tick - offsets[i])
    for copy in pending:
        copy.wait_send()


def shards(x_saved, block_scales, gate_grad, gate_weight):
    widths = [w for _, w in PIECES]
    dma = pltpu.SemaphoreType.DMA
    vmem, hbm = pl.BlockSpec(memory_space=pltpu.VMEM), pl.BlockSpec(memory_space=pl.ANY)
    n = len(PIECES)
    return pl.pallas_call(
        kernel,
        out_shape=(jax.ShapeDtypeStruct((ROWS, D), BF16), jax.ShapeDtypeStruct((28, FF), F32)),
        in_specs=[vmem, vmem, hbm, hbm],
        out_specs=(vmem, vmem),
        scratch_shapes=[
            pltpu.VMEM((NX, ROWS, DX), BF16),
            pltpu.VMEM((NX, GROUP, DX), BF16),
            pltpu.VMEM((DX, NX * GROUP), BF16),
            pltpu.VMEM((NX, GROUP, FF), BF16),
            pltpu.VMEM((D, FF), BF16),
            pltpu.VMEM((DX, FF), F32),
            pltpu.VMEM((NY * NC, ROWS, D), F32),
            pltpu.VMEM((NY, ROWS, D), F32),
            pltpu.VMEM((NY - 1, ROWS, D), BF16),
            pltpu.VMEM((NY - 1, ROWS, D), BF16),
            *[pltpu.VMEM((DZ, w), BF16) for w in widths],
            *[pltpu.VMEM((DZ, w), BF16) for w in widths],
            *[pltpu.VMEM((FWD - 1, DZ, w), BF16) for w in widths],
            *[pltpu.VMEM((BWD - 1, DZ, w), BF16) for w in widths],
            *[pltpu.VMEM((4, DZ, w), F32) for w in widths],
            *[pltpu.VMEM((DZ, w), F32) for w in widths],
            *[pltpu.VMEM((32, w), F32) for w in widths],
            dma((1 + D // WCHUNK,)),
            dma((3,)), dma((3,)), dma((3,)), dma((3,)), dma((4,)), dma((4,)),
            dma((3 * n,)), dma((3 * n,)), dma((4,)), dma((4,)), dma((3,)), dma((3,)),
            dma((FWD * n,)), dma((FWD * n,)), dma((BWD * n,)), dma((BWD * n,)), dma((n,)), dma((n,)),
        ],
        compiler_params=pltpu.CompilerParams(
            collective_id=0, has_side_effects=True, vmem_limit_bytes=56 * 2**20
        ),
        cost_estimate=pl.CostEstimate(flops=4 * GROUP * D * FF, bytes_accessed=12 * 2**20, transcendentals=0),
    )(x_saved, block_scales, gate_grad, gate_weight)


def solution(mesh):
    return jax.shard_map(
        shards,
        mesh=mesh,
        in_specs=(
            P(("dp", "tensor"), None),
            P(("dp", "tensor"), None),
            P("dp", "tensor"),
            P(None, "tensor"),
        ),
        out_specs=(P(("dp", "tensor"), None), P("dp", "tensor")),
        check_vma=False,
    )
```

time: 741 us -> 108 us (0.15)
  the two profiles are of different devices: /device:TPU:12 before, /device:TPU:8 now
where the time goes in v1:
time: 108 us
  Pallas kernels  87.9 us (81%)
  local copies, waits for them, and re-layouts  19.2 us (18%)
    pallas_call x1, Pallas kernels, shards(): pl.pallas_call(kernel, out_shape=(jax.ShapeDtypeStruct((ROWS, D), BF16),...  87.9 us
    unnamed x5, local copies, waits for them, and re-layouts  19.2 us

profile of v1, /device:TPU:8, one launch (start us, length us, event | category | flops | bytes accessed | tf_op | source)
XLA Modules:
  0.0 107.7 jit_solution(9532027810275893392)
XLA Ops:
  0.6 1.4 %copy.6.scale_ref = f32[32,21]{1,0:T(8,128)} copy(f32[32,21]{0,1:T(8,128)} %param.5) | data formatting | bytes 5376 | tf_op args[1]
  2.0 2.2 %copy.7.grad_ref = bf16[256,1600]{1,0:T(8,128)(2,1)} copy(bf16[256,1600]{0,1:T(8,128)(2,1)} %param.6) | data formatting | bytes 1638400 | tf_op args[2]
  4.2 12.4 %copy.8.weight_ref = bf16[2688,1600]{1,0:T(8,128)(2,1)} copy(bf16[2688,1600]{0,1:T(8,128)(2,1)} %param.7) | data formatting | bytes 17203200 | tf_op args[3]
  16.6 87.9 %shard_map.59 = (bf16[32,2688]{1,0:T(8,128)(2,1)}, f32[28,1600]{1,0:T(8,128)}) custom-call(bf16[32,2688]{1,0:T(8,128)(2,1)} %x_ref.1, f32[32,21]{1,0:T(8,128)} %copy.6.scale_ref, bf16[256,1600]{1,0:T(8,128)(2,1)} %copy.7.grad_ref, bf16[2688,1600]{1,0:T(8,128)(2,1)} %copy.8.weight_ref), custom_call_target="tpu_custom_call" | custom-call | flops 4404019200 | bytes 12582912 | tf_op jit(solution)/shard_map/pallas_call | solution.py:248
  104.5 1.6 %copy.11 = bf16[32,2688]{1,0:T(8,128)(2,1)} copy(bf16[32,2688]{1,0:T(8,128)(2,1)} %get-tuple-element.4) | data formatting | bytes 344064
  106.1 1.6 %copy.12 = f32[28,1600]{1,0:T(8,128)} copy(f32[28,1600]{1,0:T(8,128)} %get-tuple-element.5) | data formatting | bytes 358400

commit v2 on v0

v2 whole, which is shorter than its diff:
```python
import math

import jax
import jax.numpy as jnp
from jax import lax
from jax.experimental import pallas as pl
from jax.experimental.pallas import tpu as pltpu
from jax.sharding import PartitionSpec as P

MESH = pl.DeviceIdType.MESH
F32, BF16 = jnp.float32, jnp.bfloat16

NX, NZ, NL, NY, NC = 4, 12, 2, 4, 2
D, FF = 2688, 1600
ROWS, GROUP = 32, 256
DX, DL = D // NX, D // (NX * NZ * NL)
BLOCK = 128
PER = (16, 12)
HALF = tuple(NL * p for p in PER)
WIDTH = tuple(NZ * h for h in HALF)
UNITS = ((0, 256), (256, 256), (512, 256), (768, 256), (1024, 256), (1280, 320))
JOBS = (
    ((0,), (0,), True),
    ((0,), (1,), True),
    ((1,), (0, 1), True),
    ((0, 1), (2,), True),
    ((0, 1), (3,), True),
    ((0, 1), (4,), False),
    ((0, 1), (5,), False),
)
ORDER = (
    "pack0", "scatter0", "own0", "pack1", "scatter1", "own1", "ig0", "ig1", "ig2", "ig3", "fwd0", "ig4", "ig5",
    "rest0", "ig6", "igmate", "fwd1", "rest1", "mate01", "mate03", "fwd2", "mate11", "mate13", "fwd3", "mate02",
    "st00", "st10", "mate12", "igo1", "igo2", "igo3", "st20", "st01", "st11", "fwd4", "st30", "st21", "st02", "st12",
    "st40", "st31", "fwd5", "st22", "st03", "st13", "st41", "st32", "st50", "st23", "st04", "st14", "st60", "st42",
    "st33", "st51", "st24", "st05", "st15", "st61", "st43", "igfin", "st34", "st25", "st52", "close0", "close1",
    "st62", "st35", "st44", "fin0", "close2", "fin1", "st53", "st63", "close3", "st45", "fin2", "st54", "st64",
    "fin3", "close4", "st55", "st65", "fin4", "close5", "close6", "fin5", "fin6",
)
FWD, BWD = 6, 5
WCHUNK = 384


def job_rows(job):
    return sum(HALF[h] for h in job[0])


def job_cols(job):
    first, last = UNITS[job[1][0]], UNITS[job[1][-1]]
    return first[0], last[0] + last[1] - first[0]


def kernel(x_ref, scale_ref, grad_ref, weight_ref, ig_ref, wg_ref, *scratch):
    scratch = list(scratch)

    def take(count=None):
        if count is None:
            return scratch.pop(0)
        return [scratch.pop(0) for _ in range(count)]

    n, h2 = len(JOBS), len(HALF)
    pack, a_buf = take(h2), take(h2)
    g_buf, w_buf, part, ig_part, ig_core, ig_send, ig_recv = take(7)
    first_out, slots, last_out, last_in, total_buf, low_out, low_in = (take(n) for _ in range(7))
    (load_sem, a2a_s, a2a_r, ya_s, ya_r, ca_s, ca_r, g_s, g_r, ic_s, ic_r, iy_s, iy_r,
     z_s, z_r, l_s, l_r) = scratch

    dp, tensor = lax.axis_index("dp"), lax.axis_index("tensor")
    x, z, yl = dp // (NZ * NL), (dp // NL) % NZ, dp % NL
    yh, c = tensor // NC, tensor % NC
    s = 1 - 2 * c

    def at(x=x, z=z, yl=yl, yh=yh, c=c):
        return ((x * NZ + z) * NL + yl, yh * NC + c)

    x_to, x_from = (x + s + NX) % NX, (x - s + NX) % NX
    z_to, z_from = (z + s + NZ) % NZ, (z - s + NZ) % NZ
    y_to, y_from, y_opp = (yh + s + NY) % NY, (yh - s + NY) % NY, (yh + 2) % NY
    slot_to, slot_from = (NX + s) % NX, (NX - s) % NX
    mate = at(c=1 - c)
    x_other = [(x + k) % NX for k in range(NX)]
    y_other = [(yh + k) % NY for k in range(NY)]

    pending = []

    def send(src, dst, send_sem, recv_sem, device):
        copy = pltpu.make_async_remote_copy(
            src_ref=src, dst_ref=dst, send_sem=send_sem, recv_sem=recv_sem,
            device_id=device, device_id_type=MESH,
        )
        copy.start()
        pending.append(copy)

    def arrived(dst, sem):
        pltpu.make_async_copy(dst, dst, sem).wait()

    barrier = pltpu.get_barrier_semaphore()
    partners = [at(x=o) for o in x_other[1:]] + [at(yh=o) for o in y_other[1:]] + [
        at(z=z_to), at(z=z_from), at(yl=1 - yl), mate]
    for partner in partners:
        pl.semaphore_signal(barrier, inc=1, device_id=partner, device_id_type=MESH)

    own_grad = pltpu.make_async_copy(grad_ref, g_buf.at[0], load_sem.at[0])
    own_grad.start()
    weights = []
    for k in range(D // WCHUNK):
        cols = pl.ds(k * WCHUNK, WCHUNK)
        load = pltpu.make_async_copy(weight_ref.at[:, cols], w_buf.at[:, cols], load_sem.at[1 + k])
        load.start()
        weights.append(load)

    scale = scale_ref[...].T
    scaled = jnp.concatenate(
        [(x_ref[:, b * BLOCK:(b + 1) * BLOCK].astype(F32) * scale[:, b:b + 1]).astype(BF16)
         for b in range(D // BLOCK)],
        axis=1,
    ).astype(F32)

    def token_rows(yh, c):
        return pl.ds(pl.multiple_of((yh * NC + c) * ROWS, ROWS), ROWS)

    mine = token_rows(yh, c)

    def pack_half(h):
        for k in range(NX):
            pack[h][k] = jnp.concatenate(
                [scaled[:, k * DX + DL * j + sum(PER[:h]):k * DX + DL * j + sum(PER[:h + 1])]
                 for j in range(NZ * NL)],
                axis=1,
            ).astype(BF16)

    def scatter_half(h):
        for k in range(1, NX):
            index = 3 * h + k - 1
            send(pack[h].at[x_other[k]], a_buf[h].at[NX - k, mine], a2a_s.at[index], a2a_r.at[index],
                 at(x=x_other[k]))
        a_buf[h][0, mine] = pack[h][x]
        share(h, 0)

    def columns(p):
        return pl.ds(0, 1) if p == 0 else pl.ds(1, NX - 1)

    def share(h, p):
        block = a_buf[h].at[columns(p), mine]
        for k, target in enumerate((y_to, y_from)):
            index = h * 5 + k * 2 + p
            send(block, block, ya_s.at[index], ya_r.at[index], at(yh=target))
        send(block, block, ca_s.at[h * 2 + p], ca_r.at[h * 2 + p], mate)

    def share_rest(h):
        for k in range(1, NX):
            index = 3 * h + k - 1
            arrived(a_buf[h].at[NX - k, mine], a2a_r.at[index])
        share(h, 1)

    def to_mate(h, k):
        block = a_buf[h].at[:, token_rows((y_from, y_opp, y_to)[k - 1], c)]
        if k == 2:
            arrived(block, ya_r.at[h * 5 + 4])
        else:
            for p in (0, 1):
                part_ = a_buf[h].at[columns(p), token_rows(y_from if k == 1 else y_to, c)]
                arrived(part_, ya_r.at[h * 5 + (k // 2) * 2 + p])
        if k == 1:
            send(block, block, ya_s.at[h * 5 + 4], ya_r.at[h * 5 + 4], at(yh=y_to))
        index = 4 + h * 3 + k - 1
        send(block, block, ca_s.at[index], ca_r.at[index], mate)

    def inputs_ready(h):
        for p in (0, 1):
            arrived(a_buf[h].at[columns(p), token_rows(yh, 1 - c)], ca_r.at[h * 2 + p])
        for k, source in enumerate((y_to, y_opp, y_from)):
            arrived(a_buf[h].at[:, token_rows(source, 1 - c)], ca_r.at[4 + h * 3 + k])

    def grad_own(i):
        units = pl.ds(*UNITS[i])
        for k, (target, slot) in enumerate(((x_to, slot_from), (x_from, slot_to))):
            send(grad_ref.at[units], g_buf.at[slot, units], g_s.at[3 * i + k], g_r.at[3 * i + k], at(x=target))

    def grad_forward(i):
        units = pl.ds(*UNITS[i])
        arrived(g_buf.at[slot_from, units], g_r.at[3 * i])
        send(g_buf.at[slot_from, units], g_buf.at[2, units], g_s.at[3 * i + 2], g_r.at[3 * i + 2], at(x=x_to))

    def grad_ready(i):
        units = pl.ds(*UNITS[i])
        arrived(g_buf.at[slot_to, units], g_r.at[3 * i + 1])
        arrived(g_buf.at[2, units], g_r.at[3 * i + 2])

    def ig_chunk(k):
        if k == 0:
            own_grad.wait()
        weights[k].wait()
        cols = pl.ds(k * WCHUNK, WCHUNK)
        prod = lax.dot_general(
            g_buf[0], w_buf[:, cols], (((0,), (0,)), ((), ())), preferred_element_type=F32
        )
        ig_part[:, :, cols] = prod.reshape(NY * NC, ROWS, WCHUNK)

    def ig_to_mate():
        for k in range(NY):
            other = y_other[k]
            send(ig_part.at[other * NC + 1 - c], ig_core.at[other], ic_s.at[k], ic_r.at[k], mate)

    def ig_to_owner(k):
        other = y_other[k]
        arrived(ig_core.at[other], ic_r.at[k])
        ig_send[k - 1] = (ig_part[other * NC + c] + ig_core[other]).astype(BF16)
        send(ig_send.at[k - 1], ig_recv.at[k - 1], iy_s.at[k - 1], iy_r.at[k - 1], at(yh=other))

    def ig_finish():
        arrived(ig_core.at[yh], ic_r.at[0])
        total = ig_part[yh * NC + c] + ig_core[yh]
        for k in range(1, NY):
            arrived(ig_recv.at[k - 1], iy_r.at[k - 1])
            total = total + ig_recv[k - 1].astype(F32)
        ig_ref[...] = total.astype(BF16)

    half_seen, unit_seen = set(), set()

    def multiply(i):
        halves, units, _ = JOBS[i]
        for u in units:
            if u not in unit_seen:
                unit_seen.add(u)
                grad_ready(u)
        for h in halves:
            if h not in half_seen:
                half_seen.add(h)
                inputs_ready(h)
        cols = pl.ds(*job_cols(JOBS[i]))
        for h in halves:
            total = None
            for k in range(NX):
                prod = lax.dot_general(
                    a_buf[h][k], g_buf[k, cols], (((0,), (1,)), ((), ())), preferred_element_type=F32
                )
                total = prod if k == 0 else total + prod
            part[sum(WIDTH[:h]):sum(WIDTH[:h + 1]), cols] = total

    def own_part(i, owner):
        cols = pl.ds(*job_cols(JOBS[i]))
        blocks = [
            part[pl.ds(pl.multiple_of(sum(WIDTH[:h]) + owner * HALF[h], 8), HALF[h]), cols] for h in JOBS[i][0]
        ]
        return blocks[0] if len(blocks) == 1 else jnp.concatenate(blocks, axis=0)

    def step(i, j):
        if j == 0:
            multiply(i)
        for d, (hops, target, sign) in enumerate(((FWD, z_to, s), (BWD, z_from, -s))):
            if j >= hops:
                continue
            base, sem = d * (FWD - 1), i * (FWD + BWD) + d * FWD
            value = own_part(i, (z + sign * (hops - j) + NZ) % NZ)
            if j > 0:
                arrived(slots[i].at[base + j - 1], z_r.at[sem + j - 1])
                value = value + slots[i][base + j - 1].astype(F32)
            if j == hops - 1:
                last_out[i][d] = value.astype(last_out[i].dtype)
                src, dst = last_out[i].at[d], last_in[i].at[d]
            elif j == 0:
                first_out[i][d] = value.astype(BF16)
                src, dst = first_out[i].at[d], slots[i].at[base]
            else:
                slots[i][base + j - 1] = value.astype(BF16)
                src, dst = slots[i].at[base + j - 1], slots[i].at[base + j]
            send(src, dst, z_s.at[sem + j], z_r.at[sem + j], at(z=target))

    def low_blocks(i, low):
        base, blocks = 0, []
        for h in JOBS[i][0]:
            blocks.append(total_buf[i][pl.ds(pl.multiple_of(base + low * (8 * (h == 1) + 16 * (h == 0)), 8), 16), :])
            base += HALF[h]
        return blocks

    def close(i):
        arrived(last_in[i].at[0], z_r.at[i * (FWD + BWD) + FWD - 1])
        arrived(last_in[i].at[1], z_r.at[i * (FWD + BWD) + FWD + BWD - 1])
        total_buf[i][...] = own_part(i, z) + last_in[i][0].astype(F32) + last_in[i][1].astype(F32)
        for k, block in enumerate(low_blocks(i, 1 - yl)):
            low_out[i][16 * k:16 * k + 16, :] = block
        send(low_out[i], low_in[i], l_s.at[i], l_r.at[i], at(yl=1 - yl))

    def finish(i):
        arrived(low_in[i], l_r.at[i])
        cols = pl.ds(*job_cols(JOBS[i]))
        for k, (h, block) in enumerate(zip(JOBS[i][0], low_blocks(i, yl))):
            total = (block + low_in[i][16 * k:16 * k + 16, :]) * (1.0 / math.sqrt(GROUP * NX * NZ * NL))
            if h == 0:
                wg_ref[0:16, cols] = total
            else:
                wg_ref[16:28, cols] = jnp.where(yl == 0, total[:12], total[4:])

    def enter(h):
        if h == 0:
            pl.semaphore_wait(barrier, len(partners))
        scatter_half(h)

    def forward(i):
        grad_forward(i)
        if i + 2 < len(UNITS):
            grad_own(i + 2)

    what = dict(pack=pack_half, scatter=enter, own=grad_own, rest=share_rest, fwd=forward, mate=to_mate, ig=ig_chunk,
                igmate=ig_to_mate, igo=ig_to_owner, igfin=ig_finish, st=step, close=close, fin=finish)
    for name in ORDER:
        word = name.rstrip("0123456789")
        what[word](*(int(digit) for digit in name[len(word):]))
    for copy in pending:
        copy.wait_send()


def shards(x_saved, block_scales, gate_grad, gate_weight):
    dma = pltpu.SemaphoreType.DMA
    vmem, hbm = pl.BlockSpec(memory_space=pltpu.VMEM), pl.BlockSpec(memory_space=pl.ANY)
    n, u, hops = len(JOBS), len(UNITS), FWD + BWD
    shapes = [(job_rows(job), job_cols(job)[1]) for job in JOBS]
    lasts = [F32 if job[2] else BF16 for job in JOBS]
    return pl.pallas_call(
        kernel,
        out_shape=(jax.ShapeDtypeStruct((ROWS, D), BF16), jax.ShapeDtypeStruct((DL, FF), F32)),
        in_specs=[vmem, vmem, hbm, hbm],
        out_specs=(vmem, vmem),
        scratch_shapes=[
            *[pltpu.VMEM((NX, ROWS, w), BF16) for w in WIDTH],
            *[pltpu.VMEM((NX, GROUP, w), BF16) for w in WIDTH],
            pltpu.VMEM((NX, FF, GROUP), BF16),
            pltpu.VMEM((FF, D), BF16),
            pltpu.VMEM((DX, FF), F32),
            pltpu.VMEM((NY * NC, ROWS, D), F32),
            pltpu.VMEM((NY, ROWS, D), F32),
            pltpu.VMEM((NY - 1, ROWS, D), BF16),
            pltpu.VMEM((NY - 1, ROWS, D), BF16),
            *[pltpu.VMEM((2, *shape), BF16) for shape in shapes],
            *[pltpu.VMEM((hops - 2, *shape), BF16) for shape in shapes],
            *[pltpu.VMEM((2, *shape), last) for shape, last in zip(shapes, lasts)],
            *[pltpu.VMEM((2, *shape), last) for shape, last in zip(shapes, lasts)],
            *[pltpu.VMEM(shape, F32) for shape in shapes],
            *[pltpu.VMEM((16 * len(job[0]), shape[1]), F32) for job, shape in zip(JOBS, shapes)],
            *[pltpu.VMEM((16 * len(job[0]), shape[1]), F32) for job, shape in zip(JOBS, shapes)],
            dma((1 + D // WCHUNK,)),
            dma((6,)), dma((6,)), dma((10,)), dma((10,)), dma((10,)), dma((10,)),
            dma((3 * u,)), dma((3 * u,)), dma((4,)), dma((4,)), dma((3,)), dma((3,)),
            dma((hops * n,)), dma((hops * n,)), dma((n,)), dma((n,)),
        ],
        compiler_params=pltpu.CompilerParams(
            collective_id=0, has_side_effects=True, vmem_limit_bytes=56 * 2**20
        ),
        cost_estimate=pl.CostEstimate(flops=4 * GROUP * D * FF, bytes_accessed=12 * 2**20, transcendentals=0),
    )(x_saved, block_scales.T, gate_grad.T, gate_weight.T)


def solution(mesh):
    return jax.shard_map(
        shards,
        mesh=mesh,
        in_specs=(
            P(("dp", "tensor"), None),
            P(("dp", "tensor"), None),
            P("dp", "tensor"),
            P(None, "tensor"),
        ),
        out_specs=(P(("dp", "tensor"), None), P("dp", "tensor")),
        check_vma=False,
    )
```

time: 741 us -> 85 us (0.11)
  the two profiles are of different devices: /device:TPU:12 before, /device:TPU:8 now
where the time goes in v2:
time: 85 us; the launch traced here: 84.8 us
  Pallas kernels  81 us (95%)
  local copies, waits for them, and re-layouts  3.23 us (4%)
    pallas_call x1, Pallas kernels, shards(): pl.pallas_call(kernel, out_shape=(jax.ShapeDtypeStruct((ROWS, D), BF16),...  81 us
    unnamed x2, local copies, waits for them, and re-layouts  3.23 us

profile of v2, /device:TPU:8, one launch (start us, length us, event | category | flops | bytes accessed | tf_op | source)
XLA Modules:
  0.0 84.8 jit_solution(5343370777887463138)
XLA Ops:
  0.6 81.0 %shard_map.59 = (bf16[32,2688]{1,0:T(8,128)(2,1)}, f32[28,1600]{1,0:T(8,128)}) custom-call(bf16[32,2688]{1,0:T(8,128)(2,1)} %x_ref.1, f32[21,32]{1,0:T(8,128)} %bitcast.5, bf16[1600,256]{1,0:T(8,128)(2,1)} %bitcast.4, bf16[1600,2688]{1,0:T(8,128)(2,1)} %bitcast.3), custom_call_target="tpu_custom_call" | custom-call | flops 4404019200 | bytes 12582912 | tf_op jit(solution)/shard_map/pallas_call | solution.py:320
  81.6 1.6 %copy.8 = bf16[32,2688]{1,0:T(8,128)(2,1)} copy(bf16[32,2688]{1,0:T(8,128)(2,1)} %get-tuple-element.4) | data formatting | bytes 344064
  83.2 1.6 %copy.9 = f32[28,1600]{1,0:T(8,128)} copy(f32[28,1600]{1,0:T(8,128)} %get-tuple-element.5) | data formatting | bytes 358400

commit v3 on v2

--- a/solution.py
+++ b/solution.py
@@ -28,14 +28,15 @@
     ((0, 1), (4,), False),
     ((0, 1), (5,), False),
 )
+DUAL = (5, 6)
 ORDER = (
     "pack0", "scatter0", "own0", "pack1", "scatter1", "own1", "ig0", "ig1", "ig2", "ig3", "fwd0", "ig4", "ig5",
     "rest0", "ig6", "igmate", "fwd1", "rest1", "mate01", "mate03", "fwd2", "mate11", "mate13", "fwd3", "mate02",
     "st00", "st10", "mate12", "igo1", "igo2", "igo3", "st20", "st01", "st11", "fwd4", "st30", "st21", "st02", "st12",
-    "st40", "st31", "fwd5", "st22", "st03", "st13", "st41", "st32", "st50", "st23", "st04", "st14", "st60", "st42",
-    "st33", "st51", "st24", "st05", "st15", "st61", "st43", "igfin", "st34", "st25", "st52", "close0", "close1",
-    "st62", "st35", "st44", "fin0", "close2", "fin1", "st53", "st63", "close3", "st45", "fin2", "st54", "st64",
-    "fin3", "close4", "st55", "st65", "fin4", "close5", "close6", "fin5", "fin6",
+    "st40", "st31", "fwd5", "st22", "st03", "st13", "st41", "st32", "st50", "st04", "st14", "st23", "st60", "st42",
+    "st33", "st51", "st05", "st15", "st24", "st61", "igfin", "st43", "st34", "close0", "close1", "st52", "st25",
+    "st62", "st35", "fin0", "st44", "fin1", "close2", "st53", "st63", "close3", "st45", "fin2", "st54", "st64",
+    "fin3", "close4", "st55", "st65", "fin4", "fin5", "fin6",
 )
 FWD, BWD = 6, 5
 WCHUNK = 384
@@ -60,10 +61,11 @@
 
     n, h2 = len(JOBS), len(HALF)
     pack, a_buf = take(h2), take(h2)
-    g_buf, w_buf, part, ig_part, ig_core, ig_send, ig_recv = take(7)
+    x_buf, scale_buf, g_buf, w_buf, part, ig_part, ig_core, ig_send, ig_recv = take(9)
     first_out, slots, last_out, last_in, total_buf, low_out, low_in = (take(n) for _ in range(7))
+    value_buf = dict(zip(DUAL, take(len(DUAL))))
     (load_sem, a2a_s, a2a_r, ya_s, ya_r, ca_s, ca_r, g_s, g_r, ic_s, ic_r, iy_s, iy_r,
-     z_s, z_r, l_s, l_r) = scratch
+     z_s, z_r, l_s, l_r, o_s, o_r) = scratch
 
     dp, tensor = lax.axis_index("dp"), lax.axis_index("tensor")
     x, z, yl = dp // (NZ * NL), (dp // NL) % NZ, dp % NL
@@ -94,9 +96,15 @@
     def arrived(dst, sem):
         pltpu.make_async_copy(dst, dst, sem).wait()
 
+    loads = []
+    for k, (src, dst) in enumerate(((x_ref, x_buf), (scale_ref, scale_buf))):
+        load = pltpu.make_async_copy(src, dst, load_sem.at[1 + D // WCHUNK + k])
+        load.start()
+        loads.append(load)
+
     barrier = pltpu.get_barrier_semaphore()
     partners = [at(x=o) for o in x_other[1:]] + [at(yh=o) for o in y_other[1:]] + [
-        at(z=z_to), at(z=z_from), at(yl=1 - yl), mate]
+        at(z=z_to), at(z=z_from), at(z=z_to, yl=1 - yl), at(z=z_from, yl=1 - yl), at(yl=1 - yl), mate]
     for partner in partners:
         pl.semaphore_signal(barrier, inc=1, device_id=partner, device_id_type=MESH)
 
@@ -109,9 +117,11 @@
         load.start()
         weights.append(load)
 
-    scale = scale_ref[...].T
+    for load in loads:
+        load.wait()
+    scale = scale_buf[...].T
     scaled = jnp.concatenate(
-        [(x_ref[:, b * BLOCK:(b + 1) * BLOCK].astype(F32) * scale[:, b:b + 1]).astype(BF16)
+        [(x_buf[:, b * BLOCK:(b + 1) * BLOCK].astype(F32) * scale[:, b:b + 1]).astype(BF16)
          for b in range(D // BLOCK)],
         axis=1,
     ).astype(F32)
@@ -248,6 +258,9 @@
     def step(i, j):
         if j == 0:
             multiply(i)
+            if i in DUAL:
+                total_buf[i][...] = own_part(i, z)
+                low_send(i)
         for d, (hops, target, sign) in enumerate(((FWD, z_to, s), (BWD, z_from, -s))):
             if j >= hops:
                 continue
@@ -256,6 +269,9 @@
             if j > 0:
                 arrived(slots[i].at[base + j - 1], z_r.at[sem + j - 1])
                 value = value + slots[i][base + j - 1].astype(F32)
+            if j == hops - 1 and i in DUAL:
+                last_both(i, d, value, target, sem + j)
+                continue
             if j == hops - 1:
                 last_out[i][d] = value.astype(last_out[i].dtype)
                 src, dst = last_out[i].at[d], last_in[i].at[d]
@@ -267,26 +283,48 @@
                 src, dst = slots[i].at[base + j - 1], slots[i].at[base + j]
             send(src, dst, z_s.at[sem + j], z_r.at[sem + j], at(z=target))
 
-    def low_blocks(i, low):
+    def low_blocks(i, ref, low):
         base, blocks = 0, []
         for h in JOBS[i][0]:
-            blocks.append(total_buf[i][pl.ds(pl.multiple_of(base + low * (8 * (h == 1) + 16 * (h == 0)), 8), 16), :])
+            blocks.append(ref[pl.ds(pl.multiple_of(base + low * (8 * (h == 1) + 16 * (h == 0)), 8), 16), :])
             base += HALF[h]
         return blocks
+
+    def low_send(i):
+        for k, block in enumerate(low_blocks(i, total_buf[i], 1 - yl)):
+            low_out[i][16 * k:16 * k + 16, :] = block
+        send(low_out[i], low_in[i], l_s.at[i], l_r.at[i], at(yl=1 - yl))
+
+    def last_both(i, d, value, target, sem):
+        scratch_ = value_buf[i].at[d]
+        scratch_[...] = value
+        for q, low in enumerate((yl, 1 - yl)):
+            for k, block in enumerate(low_blocks(i, scratch_, low)):
+                last_out[i][d, q, 16 * k:16 * k + 16, :] = block.astype(BF16)
+            index = 2 * DUAL.index(i) + d
+            ss, rs = (z_s.at[sem], z_r.at[sem]) if q == 0 else (o_s.at[index], o_r.at[index])
+            send(last_out[i].at[d, q], last_in[i].at[d, q], ss, rs, at(z=target, yl=low))
 
     def close(i):
         arrived(last_in[i].at[0], z_r.at[i * (FWD + BWD) + FWD - 1])
         arrived(last_in[i].at[1], z_r.at[i * (FWD + BWD) + FWD + BWD - 1])
         total_buf[i][...] = own_part(i, z) + last_in[i][0].astype(F32) + last_in[i][1].astype(F32)
-        for k, block in enumerate(low_blocks(i, 1 - yl)):
-            low_out[i][16 * k:16 * k + 16, :] = block
-        send(low_out[i], low_in[i], l_s.at[i], l_r.at[i], at(yl=1 - yl))
+        low_send(i)
 
     def finish(i):
         arrived(low_in[i], l_r.at[i])
+        extra = None
+        if i in DUAL:
+            for d, hops in enumerate((FWD, BWD)):
+                arrived(last_in[i].at[d, 0], z_r.at[i * (FWD + BWD) + d * FWD + hops - 1])
+                arrived(last_in[i].at[d, 1], o_r.at[2 * DUAL.index(i) + d])
+            extra = sum(last_in[i][d, q].astype(F32) for d in (0, 1) for q in (0, 1))
         cols = pl.ds(*job_cols(JOBS[i]))
-        for k, (h, block) in enumerate(zip(JOBS[i][0], low_blocks(i, yl))):
-            total = (block + low_in[i][16 * k:16 * k + 16, :]) * (1.0 / math.sqrt(GROUP * NX * NZ * NL))
+        for k, (h, block) in enumerate(zip(JOBS[i][0], low_blocks(i, total_buf[i], yl))):
+            total = block + low_in[i][16 * k:16 * k + 16, :]
+            if extra is not None:
+                total = total + extra[16 * k:16 * k + 16]
+            total = total * (1.0 / math.sqrt(GROUP * NX * NZ * NL))
             if h == 0:
                 wg_ref[0:16, cols] = total
             else:
@@ -316,15 +354,18 @@
     vmem, hbm = pl.BlockSpec(memory_space=pltpu.VMEM), pl.BlockSpec(memory_space=pl.ANY)
     n, u, hops = len(JOBS), len(UNITS), FWD + BWD
     shapes = [(job_rows(job), job_cols(job)[1]) for job in JOBS]
+    last_shapes = [(2, 2, 32, shape[1]) if i in DUAL else (2, *shape) for i, shape in enumerate(shapes)]
     lasts = [F32 if job[2] else BF16 for job in JOBS]
     return pl.pallas_call(
         kernel,
-        out_shape=(jax.ShapeDtypeStruct((ROWS, D), BF16), jax.ShapeDtypeStruct((DL, FF), F32)),
-        in_specs=[vmem, vmem, hbm, hbm],
+        out_shape=(pltpu.VMEM((ROWS, D), BF16), pltpu.VMEM((DL, FF), F32)),
+        in_specs=[hbm, hbm, hbm, hbm],
         out_specs=(vmem, vmem),
         scratch_shapes=[
             *[pltpu.VMEM((NX, ROWS, w), BF16) for w in WIDTH],
             *[pltpu.VMEM((NX, GROUP, w), BF16) for w in WIDTH],
+            pltpu.VMEM((ROWS, D), BF16),
+            pltpu.VMEM((D // BLOCK, ROWS), F32),
             pltpu.VMEM((NX, FF, GROUP), BF16),
             pltpu.VMEM((FF, D), BF16),
             pltpu.VMEM((DX, FF), F32),
@@ -334,15 +375,17 @@
             pltpu.VMEM((NY - 1, ROWS, D), BF16),
             *[pltpu.VMEM((2, *shape), BF16) for shape in shapes],
             *[pltpu.VMEM((hops - 2, *shape), BF16) for shape in shapes],
-            *[pltpu.VMEM((2, *shape), last) for shape, last in zip(shapes, lasts)],
-            *[pltpu.VMEM((2, *shape), last) for shape, last in zip(shapes, lasts)],
+            *[pltpu.VMEM(shape, last) for shape, last in zip(last_shapes, lasts)],
+            *[pltpu.VMEM(shape, last) for shape, last in zip(last_shapes, lasts)],
             *[pltpu.VMEM(shape, F32) for shape in shapes],
             *[pltpu.VMEM((16 * len(job[0]), shape[1]), F32) for job, shape in zip(JOBS, shapes)],
             *[pltpu.VMEM((16 * len(job[0]), shape[1]), F32) for job, shape in zip(JOBS, shapes)],
-            dma((1 + D // WCHUNK,)),
+            *[pltpu.VMEM((2, *shapes[i]), F32) for i in DUAL],
+            dma((3 + D // WCHUNK,)),
             dma((6,)), dma((6,)), dma((10,)), dma((10,)), dma((10,)), dma((10,)),
             dma((3 * u,)), dma((3 * u,)), dma((4,)), dma((4,)), dma((3,)), dma((3,)),
             dma((hops * n,)), dma((hops * n,)), dma((n,)), dma((n,)),
+            dma((2 * len(DUAL),)), dma((2 * len(DUAL),)),
         ],
         compiler_params=pltpu.CompilerParams(
             collective_id=0, has_side_effects=True, vmem_limit_bytes=56 * 2**20

time: 85 us -> 79.2 us (0.932)
  Pallas kernels: 81 us -> 77.1 us
  local copies, waits for them, and re-layouts: 3.23 us -> 1.35 us
    pallas_call x1, Pallas kernels: 81 us -> 77.1 us  [shards(): pl.pallas_call(kernel, out_shape=(pltpu.VMEM((ROWS, D), BF16), pltpu.VMEM...]
    unnamed x2, local copies, waits for them, and re-layouts: 3.23 us -> 1.35 us
where the time goes in v3:
time: 79.2 us; the launch traced here: 79.1 us
  Pallas kernels  77.1 us (97%)
  local copies, waits for them, and re-layouts  1.35 us (2%)
    pallas_call x1, Pallas kernels, shards(): pl.pallas_call(kernel, out_shape=(pltpu.VMEM((ROWS, D), BF16), pltpu.VMEM...  77.1 us

profile of v3, /device:TPU:8, one launch (start us, length us, event | category | flops | bytes accessed | tf_op | source)
XLA Modules:
  0.0 79.1 jit_solution(8574258478327305507)
XLA Ops:
  0.6 77.1 %shard_map.59 = (bf16[32,2688]{1,0:T(8,128)(2,1)S(1)}, f32[28,1600]{1,0:T(8,128)S(1)}) custom-call(bf16[32,2688]{1,0:T(8,128)(2,1)} %x_ref.1, f32[21,32]{1,0:T(8,128)} %bitcast.5, bf16[1600,256]{1,0:T(8,128)(2,1)} %bitcast.4, bf16[1600,2688]{1,0:T(8,128)(2,1)} %bitcast.3), custom_call_target="tpu_custom_call" | custom-call | flops 4404019200 | bytes 12582912 | tf_op jit(solution)/shard_map/pallas_call | solution.py:359
  77.7 0.7 copy.8
  78.4 0.7 copy.9

commit v4 on v3

--- a/solution.py
+++ b/solution.py
@@ -76,7 +76,7 @@
         return ((x * NZ + z) * NL + yl, yh * NC + c)
 
     x_to, x_from = (x + s + NX) % NX, (x - s + NX) % NX
-    z_to, z_from = (z + s + NZ) % NZ, (z - s + NZ) % NZ
+    z_to, z_from = (z - s + NZ) % NZ, (z + s + NZ) % NZ
     y_to, y_from, y_opp = (yh + s + NY) % NY, (yh - s + NY) % NY, (yh + 2) % NY
     slot_to, slot_from = (NX + s) % NX, (NX - s) % NX
     mate = at(c=1 - c)
@@ -261,7 +261,7 @@
             if i in DUAL:
                 total_buf[i][...] = own_part(i, z)
                 low_send(i)
-        for d, (hops, target, sign) in enumerate(((FWD, z_to, s), (BWD, z_from, -s))):
+        for d, (hops, target, sign) in enumerate(((FWD, z_to, -s), (BWD, z_from, s))):
             if j >= hops:
                 continue
             base, sem = d * (FWD - 1), i * (FWD + BWD) + d * FWD

time: 79.2 us -> 77.9 us (0.984)
  Pallas kernels: 77.1 us -> 75.8 us
    pallas_call x1, Pallas kernels: 77.1 us -> 75.8 us  [shards(): pl.pallas_call(kernel, out_shape=(pltpu.VMEM((ROWS, D), BF16), pltpu.VMEM...]
where the time goes in v4:
time: 77.9 us; the launch traced here: 77.8 us
  Pallas kernels  75.8 us (97%)
  local copies, waits for them, and re-layouts  1.35 us (2%)
    pallas_call x1, Pallas kernels, shards(): pl.pallas_call(kernel, out_shape=(pltpu.VMEM((ROWS, D), BF16), pltpu.VMEM...  75.8 us

profile of v4, /device:TPU:8, one launch (start us, length us, event | category | flops | bytes accessed | tf_op | source)
XLA Modules:
  0.0 77.8 jit_solution(13540231995909660570)
XLA Ops:
  0.6 75.8 %shard_map.59 = (bf16[32,2688]{1,0:T(8,128)(2,1)S(1)}, f32[28,1600]{1,0:T(8,128)S(1)}) custom-call(bf16[32,2688]{1,0:T(8,128)(2,1)} %x_ref.1, f32[21,32]{1,0:T(8,128)} %bitcast.5, bf16[1600,256]{1,0:T(8,128)(2,1)} %bitcast.4, bf16[1600,2688]{1,0:T(8,128)(2,1)} %bitcast.3), custom_call_target="tpu_custom_call" | custom-call | flops 4404019200 | bytes 12582912 | tf_op jit(solution)/shard_map/pallas_call | solution.py:359
  76.4 0.7 copy.8
  77.1 0.7 copy.9
